TPU v7x, 32 devices: a whole 2x2x4 slice. The times are simulated.
32 devices in a mesh: section: 4 (over y, x), seq: 2 (over core), head: 4 (over z).
Axes of the slice: x: 2, y: 2, z: 4, core: 2. Of those that a mesh axis runs over, the one named last changes fastest.
Arguments:
- encoder_states: bfloat16 [4, 2048, 4096], P(None, 'seq'), may hold values from -6 to 6
- w_kv: bfloat16 [4, 4096, 4096], P(None, None, ('section', 'head')), may hold values from -0.125 to 0.125
- queries: bfloat16 [4, 4, 256, 4, 512], P('section', None, None, None, 'head'), may hold values from -102 to 102
- cotangent: bfloat16 [4, 4, 256, 4, 512], P('section', None, None, None, 'head'), may hold values from -6 to 6
- src_len: int32 [4], replicated, may hold values from 512 to 2048, as said below
- tgt_len: int32 [4], replicated, may hold values from 64 to 256, as said below
Outputs:
- attn_out: bfloat16 [4, 4, 256, 4, 512], P('section', None, 'seq', None, 'head')
- query_grads: bfloat16 [4, 4, 256, 4, 512], P('section', None, 'seq', None, 'head')
- source_grads: bfloat16 [4, 2048, 4096], P(None, 'seq', ('section', 'head'))
Inputs may be any that keep to these rules, and one draw needn't show every extreme that they name: `src_len`: at least one sample has all 2048 source tokens. `tgt_len`: at least one sample has all 256 target tokens.
All inputs are finite; a program needn't handle non-finite values.
Results may differ from a plain program's by a relative error of at most 0.014.
The roundings to bfloat16 on the way count: a program that leaves them out, or rounds other values in their place, can miss the bound.
Values may be sent and summed in bfloat16 or wider, within the bound.
A program may use at most 192 MiB of HBM per device.

v0:
```python
import jax
import jax.numpy as jnp
from jax import lax
from jax.sharding import PartitionSpec as P

masked_score = -1e30


def body(encoder_states, w_kv, queries, cotangent, src_len, tgt_len):
    sections = lax.axis_size("section")
    shards = lax.axis_size("seq")
    seat = lax.axis_index("seq")
    samples = encoder_states.shape[0]
    src_rows = encoder_states.shape[1]
    model_width = encoder_states.shape[2]
    layers = w_kv.shape[0]
    pair_cols = w_kv.shape[2]
    head_dim = pair_cols // 2
    piece_len = src_rows // shards
    groups = queries.shape[3]
    target_rows = queries.shape[2]
    key_count = shards * piece_len
    score_scale = head_dim ** (-0.5)
    local_source = encoder_states.reshape(samples, shards, piece_len, model_width)
    projected = jnp.einsum(
        "bqpd,ldc->lqbpc", local_source, w_kv, preferred_element_type=jnp.float32
    ).astype(jnp.bfloat16)
    moved = lax.all_to_all(
        projected.reshape(layers * shards, samples, piece_len, pair_cols),
        ("section", "seq"),
        split_axis=0,
        concat_axis=0,
        tiled=True,
    )
    moved = moved.reshape(sections, shards, samples, piece_len, pair_cols)
    key_rows = moved[..., :head_dim]
    value_rows = moved[..., head_dim:]
    query_now = queries[0]
    scores = jnp.einsum(
        "btgd,gqbpd->gbtqp", query_now, key_rows, preferred_element_type=jnp.float32
    )
    scores = scores.reshape(groups, samples, target_rows, key_count) * score_scale
    position = (
        jnp.arange(shards, dtype=jnp.int32)[:, None] * src_rows
        + seat * piece_len
        + jnp.arange(piece_len, dtype=jnp.int32)[None, :]
    )
    position = position.reshape(key_count)
    key_live = position[None, :] < src_len[:, None]
    scores = jnp.where(key_live[None, :, None, :], scores, masked_score)
    row_top = lax.pmax(jnp.max(scores, axis=-1), "seq")
    exponent = jnp.exp(scores - row_top[..., None])
    row_total = lax.psum(jnp.sum(exponent, axis=-1), "seq")
    probability = exponent / row_total[..., None]
    probability_low = probability.astype(jnp.bfloat16)
    blocks_low = probability_low.reshape(groups, samples, target_rows, shards, piece_len)
    part_out = jnp.einsum(
        "gbtqp,gqbpd->btgd", blocks_low, value_rows, preferred_element_type=jnp.float32
    )
    query_live = jnp.arange(target_rows, dtype=jnp.int32)[None, :] < tgt_len[:, None]
    grad_low = jnp.where(query_live[:, :, None, None], cotangent[0], jnp.zeros((), jnp.bfloat16))
    grad_probs = jnp.einsum(
        "btgd,gqbpd->gbtqp", grad_low, value_rows, preferred_element_type=jnp.float32
    )
    grad_probs = grad_probs.reshape(groups, samples, target_rows, key_count)
    own_out = lax.psum_scatter(part_out, "seq", scatter_dimension=1, tiled=True)
    row_delta = lax.psum(jnp.sum(probability_low.astype(jnp.float32) * grad_probs, axis=-1), "seq")
    grad_scores = (probability * (grad_probs - row_delta[..., None])).astype(jnp.bfloat16)
    grad_scores = grad_scores.reshape(groups, samples, target_rows, shards, piece_len)
    part_query = score_scale * jnp.einsum(
        "gbtqp,gqbpd->btgd", grad_scores, key_rows, preferred_element_type=jnp.float32
    )
    own_query = lax.psum_scatter(part_query, "seq", scatter_dimension=1, tiled=True)
    grad_keys = score_scale * jnp.einsum(
        "gbtqp,btgd->gqbpd", grad_scores, query_now, preferred_element_type=jnp.float32
    )
    grad_values = jnp.einsum(
        "gbtqp,btgd->gqbpd", blocks_low, grad_low, preferred_element_type=jnp.float32
    )
    grad_pairs = jnp.concatenate([grad_keys, grad_values], axis=-1).astype(jnp.bfloat16)
    returned = lax.all_to_all(
        grad_pairs.reshape(sections * shards, samples, piece_len, pair_cols),
        ("section", "seq"),
        split_axis=0,
        concat_axis=0,
        tiled=True,
    )
    returned = returned.reshape(layers, shards, samples, piece_len, pair_cols)
    source_terms = jnp.einsum("lqbpc,ldc->bqpd", returned, w_kv, preferred_element_type=jnp.float32)
    source_terms = source_terms.reshape(samples, src_rows, model_width)
    source_part = lax.psum_scatter(
        source_terms, ("section", "head"), scatter_dimension=2, tiled=True
    )
    return (
        own_out.astype(jnp.bfloat16)[None],
        own_query.astype(jnp.bfloat16)[None],
        source_part.astype(jnp.bfloat16),
    )


def solution(mesh):
    placed = (
        P(None, "seq", None),
        P(None, None, ("section", "head")),
        P("section", None, None, None, "head"),
        P("section", None, None, None, "head"),
        P(),
        P(),
    )
    return jax.shard_map(
        body,
        mesh=mesh,
        in_specs=placed,
        out_specs=(
            P("section", None, "seq", None, "head"),
            P("section", None, "seq", None, "head"),
            P(None, "seq", ("section", "head")),
        ),
        check_vma=False,
    )
```

profile of v0, /device:TPU:0, one launch (start us, length us, event | category | flops | bytes accessed | tf_op | source)
XLA Modules:
  0.0 1783.4 jit_solution(8734368526237635077)
XLA Ops:
  7.2 42.7 %convert_bitcast_fusion = bf16[4,2,4,512,256]{3,4,1,2,0:T(8,128)(2,1)} fusion(bf16[4,2,512,4096,1]{3,2,1,0,4:T(8,128)(2,1)} %bitcast.83, bf16[4,4096,256]{2,1,0:T(8,128)(2,1)} %param.7), kind=kOutput, calls=%fused_computation.19 | convolution fusion | flops 34363932672 | bytes 50331648 | tf_op jit(solution)/shard_map/bqpd,ldc->lqbpc/dot_general | solution.py:25
  49.9 13.2 copy.25
  63.1 5.3 all-to-all-start
  68.5 1.9 fusion.32
  70.5 0.7 copy.58
  71.1 0.7 copy.57
  72.0 90.9 %all-to-all-done = bf16[8,4,512,256]{3,2,1,0:T(8,128)(2,1)} async-done(((bf16[8,4,512,256]{3,2,1,0:T(8,128)(2,1)}), bf16[8,4,512,256]{3,2,1,0:T(8,128)(2,1)}, u32[]{:S(2)}, u32[]{:S(2)}) %all-to-all-start) | async-done | bytes 8388640 | tf_op jit(solution)/shard_map/all_to_all | solution.py:28
  162.9 5.3 fusion.34
  168.2 7.2 bitcast_reduce_fusion
  175.4 3.5 pmax.7
  178.9 7.7 fusion.2
  186.7 3.5 psum.14
  190.2 15.2 multiply_reduce_fusion
  205.4 3.3 psum.15
  208.7 14.9 multiply_convert_fusion
  223.6 8.2 fusion.14
  231.8 7.3 copy.38
  239.0 8.1 convert_bitcast_fusion.1
  247.2 7.3 copy.41
  254.5 7.7 pad_maximum_fusion
  262.2 4.9 all-to-all-start.1
  267.2 0.3 reduce-scatter.6.cloned.1.call-start
  267.4 7.6 fusion.22
  275.1 7.6 fusion.23
  282.7 78.5 %all-to-all-done.1 = bf16[8,4,512,256]{3,2,1,0:T(8,128)(2,1)} async-done(((bf16[8,4,512,256]{3,2,1,0:T(8,128)(2,1)}), bf16[8,4,512,256]{3,2,1,0:T(8,128)(2,1)}, u32[]{:S(2)}, u32[]{:S(2)}) %all-to-all-start.1) | async-done | bytes 8388640 | tf_op jit(solution)/shard_map/all_to_all | solution.py:81
  361.2 45.5 %fusion.5 = f32[2,4,512,4096,1]{3,2,0,1,4:T(8,128)} fusion(bf16[4,4096,256]{2,1,0:T(8,128)(2,1)} %param.7, bf16[4,2,4,512,256]{4,3,2,1,0:T(8,128)(2,1)} %bitcast.25), kind=kOutput, calls=%fused_computation.11 | convolution fusion | flops 34359738368 | bytes 83886080 | tf_op jit(solution)/shard_map/lqbpc,ldc->bqpd/dot_general | solution.py:89
  406.8 1.3 convert_bitcast_fusion.2
  408.1 1.1 copy.45
  409.1 1.3 convert_bitcast_fusion.3
  410.5 1.1 copy.44
  411.5 1361.7 %reduce-scatter.8.cloned.1.call-done = f32[4,1024,256]{2,1,0:T(8,128)} async-done(((f32[4,1024,4096]{2,1,0:T(8,128)}), f32[4,1024,256]{2,1,0:T(8,128)}) %reduce-scatter.8.cloned.1.call-update) | async-done | bytes 4194320 | tf_op jit(solution)/shard_map/reduce_scatter | solution.py:91
  1773.2 3.7 convert_element_type.37
  (21 shorter events, 0.4 us)
Async XLA Ops:
  63.1 5.3 copy-start.4
  63.1 5.4 copy-start.2
  63.1 8.0 copy-start.1
  63.1 8.8 copy-start.3
  63.1 99.8 %all-to-all-start = ((bf16[8,4,512,256]{3,2,1,0:T(8,128)(2,1)}), bf16[8,4,512,256]{3,2,1,0:T(8,128)(2,1)}, u32[]{:S(2)}, u32[]{:S(2)}) async-start(bf16[8,4,512,256]{3,2,1,0:T(8,128)(2,1)} %bitcast.79), calls=%async_computation | async-start | bytes 16777216 | tf_op jit(solution)/shard_map/all_to_all | solution.py:28
  168.2 7.2 copy-start
  262.2 99.0 %all-to-all-start.1 = ((bf16[8,4,512,256]{3,2,1,0:T(8,128)(2,1)}), bf16[8,4,512,256]{3,2,1,0:T(8,128)(2,1)}, u32[]{:S(2)}, u32[]{:S(2)}) async-start(bf16[8,4,512,256]{3,2,1,0:T(8,128)(2,1)} %pad_maximum_fusion), calls=%async_computation.3 | async-start | bytes 16777216 | tf_op jit(solution)/shard_map/all_to_all | solution.py:81
  267.2 139.6 %reduce-scatter.6.cloned.1.call-start = ((), (), s32[]{:S(2)}) async-start(), calls=%async_computation.6 | async-start | bytes 3145728 | tf_op jit(solution)/shard_map/reduce_scatter | solution.py:73
  275.0 134.1 %reduce-scatter.4.cloned.1.call-start = ((), (), s32[]{:S(2)}) async-start(), calls=%async_computation.5 | async-start | bytes 3145728 | tf_op jit(solution)/shard_map/reduce_scatter | solution.py:66
  282.7 1490.5 %reduce-scatter.8.cloned.1.call-start = ((), (), s32[]{:S(2)}) async-start(), calls=%async_computation.7 | async-start | bytes 71303168 | tf_op jit(solution)/shard_map/reduce_scatter | solution.py:91
Sparse Core Ops, SparseCore 0:
  275.2 11.7 reduce-scatter.5
  289.9 10.8 reduce-scatter.3
  406.8 1366.2 reduce-scatter.7
where the time goes:
time: 1780 us
  waiting for transfers between devices  1530 us (86%)
  matrix products  142 us (8%)
  other arithmetic  38.9 us (2%)
  local copies, waits for them, and re-layouts  36.5 us (2%)
    reduce_scatter x1, waiting for transfers between devices, body(): lax.psum_scatter(source_terms, ('section', 'head'), scatter_dimension=2,...  1360 us
    all_to_all x1, waiting for transfers between devices, body(): lax.all_to_all(projected.reshape(layers * shards, samples, piece_len, pai...  90.9 us
    all_to_all x1, waiting for transfers between devices, body(): lax.all_to_all(grad_pairs.reshape(sections * shards, samples, piece_len,...  78.5 us
    dot_general x1, matrix products, body(): jnp.einsum('lqbpc,ldc->bqpd', returned, w_kv, preferred_element_type=jnp....  45.5 us
    dot_general x1, matrix products, body(): jnp.einsum('bqpd,ldc->lqbpc', local_source, w_kv, preferred_element_type=...  42.7 us
  transfers between devices with their start and end apart: 5, of which 3 were waited for; matrix products, arithmetic and copies ran while one was open for 4% of the time, Pallas kernels for 0%

commit v1 on v0

v1 whole, which is shorter than its diff:
```python
import jax
import jax.numpy as jnp
from jax import lax
from jax.sharding import PartitionSpec as P

masked_score = -1e30


def shifted(x, axis, k):
    size = lax.axis_size(axis)
    return lax.ppermute(x, axis, [(i, (i + k) % size) for i in range(size)])


def gathered(x, axis):
    size, me = lax.axis_size(axis), lax.axis_index(axis)
    full = jnp.zeros((size,) + x.shape, x.dtype)
    for k in range(size):
        block = x if k == 0 else shifted(x, axis, k)
        full = lax.dynamic_update_index_in_dim(full, block, lax.rem(me - k + size, size), 0)
    return full


def merged(stat, axis):
    size = lax.axis_size(axis)
    parts = [stat] + [shifted(stat, axis, k) for k in range(1, size)]
    top = parts[0][0]
    for part in parts[1:]:
        top = jnp.maximum(top, part[0])
    total = sum(jnp.exp(part[0] - top) * part[1] for part in parts)
    inner = sum(jnp.exp(part[0] - top) * part[2] for part in parts)
    return jnp.stack([top, total, inner])


def summed(pick, axis):
    size, me = lax.axis_size(axis), lax.axis_index(axis)
    held = pick(me).astype(jnp.float32)
    for k in range(1, size):
        held = held + shifted(pick(lax.rem(me + k, size)), axis, k).astype(jnp.float32)
    return held.astype(jnp.bfloat16)


def body(encoder_states, w_kv, queries, cotangent, src_len, tgt_len):
    f32, bf16 = jnp.float32, jnp.bfloat16
    sections = lax.axis_size("section")
    shards = lax.axis_size("seq")
    heads = lax.axis_size("head")
    section = lax.axis_index("section")
    seat = lax.axis_index("seq")
    samples, src_rows, model_width = encoder_states.shape
    layers = w_kv.shape[0]
    pair_cols = w_kv.shape[2]
    head_dim = pair_cols // 2
    chunk = src_rows // sections
    groups = queries.shape[3]
    target_rows = queries.shape[2]
    own_rows = target_rows // shards
    width = model_width // (sections * heads)
    score_scale = head_dim ** (-0.5)

    query_live = jnp.arange(target_rows, dtype=jnp.int32)[None, :] < tgt_len[:, None]
    grad_own = jnp.where(query_live[:, :, None, None], cotangent[0], jnp.zeros((), bf16))
    rows_own = jnp.stack([queries[0], grad_own]).transpose(0, 1, 3, 2, 4)
    rows_own = lax.dynamic_slice_in_dim(rows_own, seat * own_rows, own_rows, axis=3)
    rows_all = lax.all_gather(gathered(rows_own, "section"), "seq", axis=4, tiled=True)
    query_all, grad_all = rows_all[:, 0], rows_all[:, 1]

    share = model_width // shards
    share_of = lax.dynamic_slice_in_dim(w_kv, seat * share, share, axis=1)
    weights = []
    for l in range(layers):
        part = gathered(share_of[l], "section")
        weights.append(lax.all_gather(part, "seq", axis=0, tiled=False))

    source = lax.dynamic_slice_in_dim(encoder_states, section * chunk, chunk, axis=1)
    source = source.reshape(samples, chunk, shards, share)
    position = seat * src_rows + section * chunk + jnp.arange(chunk, dtype=jnp.int32)
    key_live = position[None, :] < src_len[:, None]

    keys, values, exps, grads, factors, deltas = [], [], [], [], [], []
    for l in range(layers):
        pair = jnp.einsum(
            "bpqd,qgdc->gbpc", source, weights[l], preferred_element_type=f32
        ).astype(bf16)
        key, value = pair[..., :head_dim], pair[..., head_dim:]
        s = jnp.einsum("bgtd,gbpd->gbtp", query_all[l], key, preferred_element_type=f32) * score_scale
        s = jnp.where(key_live[None, :, None, :], s, masked_score)
        top = jnp.max(s, axis=-1)
        e = jnp.exp(s - top[..., None])
        gp = jnp.einsum("bgtd,gbpd->gbtp", grad_all[l], value, preferred_element_type=f32)
        mine = jnp.stack([top, jnp.sum(e, axis=-1), jnp.sum(e * gp, axis=-1)])
        whole = merged(merged(mine, "seq"), "section")
        factors.append(jnp.exp(top - whole[0]) / whole[1])
        deltas.append(whole[2] / whole[1])
        keys.append(key)
        values.append(value)
        exps.append(e)
        grads.append(gp)

    results, pairs = [], []
    for l in range(layers):
        p = exps[l] * factors[l][..., None]
        low = p.astype(bf16)
        ds = (p * (grads[l] - deltas[l][..., None])).astype(bf16)
        out = jnp.einsum("gbtp,gbpd->gbtd", low, values[l], preferred_element_type=f32)
        dq = score_scale * jnp.einsum("gbtp,gbpd->gbtd", ds, keys[l], preferred_element_type=f32)
        results.append(jnp.stack([out.astype(bf16), dq.astype(bf16)]))
        gk = score_scale * jnp.einsum("gbtp,bgtd->gbpd", ds, query_all[l], preferred_element_type=f32)
        gv = jnp.einsum("gbtp,bgtd->gbpd", low, grad_all[l], preferred_element_type=f32)
        pairs.append(jnp.concatenate([gk, gv], axis=-1).astype(bf16))

    result = jnp.stack(results)
    result = summed(
        lambda i: lax.dynamic_slice_in_dim(result, i * own_rows, own_rows, axis=4), "seq"
    )
    result = summed(lambda i: lax.dynamic_index_in_dim(result, i, 0, keepdims=False), "section")
    result = result.transpose(0, 2, 3, 1, 4)

    source_part = jnp.zeros((samples, src_rows, width), bf16)
    for b in range(samples):
        term = sum(
            jnp.einsum("gpc,qgdc->pqd", pairs[l][:, b], weights[l], preferred_element_type=f32)
            for l in range(layers)
        )
        term = term.astype(bf16).reshape(chunk, model_width)

        def pick(h, term=term):
            return jnp.stack(
                [
                    lax.dynamic_slice_in_dim(term, (s * heads + h) * width, width, axis=1)
                    for s in range(sections)
                ]
            )

        total = summed(pick, "head")
        for k in range(sections):
            block = lax.dynamic_index_in_dim(total, lax.rem(section + k, sections), 0)
            if k:
                block = shifted(block, "section", k)
            owner = lax.rem(section - k + sections, sections)
            source_part = lax.dynamic_update_slice(source_part, block, (b, owner * chunk, 0))
    return result[0][None], result[1][None], source_part


def solution(mesh):
    placed = (
        P(None, "seq", None),
        P(None, None, ("section", "head")),
        P("section", None, None, None, "head"),
        P("section", None, None, None, "head"),
        P(),
        P(),
    )
    return jax.shard_map(
        body,
        mesh=mesh,
        in_specs=placed,
        out_specs=(
            P("section", None, "seq", None, "head"),
            P("section", None, "seq", None, "head"),
            P(None, "seq", ("section", "head")),
        ),
        check_vma=False,
    )
```

time: 1780 us -> 837 us (0.47)
  waiting for transfers between devices: 1530 us -> 263 us
  local copies, waits for them, and re-layouts: 36.5 us -> 164 us
  starting transfers between devices: 10.6 us -> 122 us
  matrix products: 142 us -> 213 us
    reduce_scatter x3 -> x0, waiting for transfers between devices: 1360 us -> none  [the longest x1 1360 us: body(): lax.psum_scatter(source_terms, ('section', 'head'), scatter_dimension=2,...]
    ppermute x0 -> x59, waiting for transfers between devices: none -> 263 us  [shifted(): return lax.ppermute(x, axis, [(i, (i + k) % size) for i in range(size)])]
    all_to_all x2 -> x0, waiting for transfers between devices: 169 us -> none  [the longest x1 90.9 us: body(): lax.all_to_all(projected.reshape(layers * shards, samples, piece_len, pai...]
    ppermute x0 -> x59, starting transfers between devices: none -> 122 us  [shifted(): return lax.ppermute(x, axis, [(i, (i + k) % size) for i in range(size)])]
    dynamic_slice x0 -> x72, local copies, waits for them, and re-layouts: none -> 78.3 us  [the longest x66 64.7 us: pick(): lax.dynamic_slice_in_dim(term, (s * heads + h) * width, width, axis=1)]
    dot_general x8 -> x44, matrix products: 142 us -> 213 us  [the longest x16 84 us: body(): jnp.einsum('gpc,qgdc->pqd', pairs[l][:, b], weights[l], preferred_element...]
    dynamic_update_slice x0 -> x31, local copies, waits for them, and re-layouts: none -> 26.2 us  [the longest x19 25.1 us: gathered(): lax.dynamic_update_index_in_dim(full, block, lax.rem(me - k + size, size)...]
    unnamed x12 -> x216, local copies, waits for them, and re-layouts: 2.15 us -> 27.2 us
  transfers between devices with their start and end apart: 5 -> 64, of which waited for: 3 -> 22; matrix products, arithmetic and copies ran while one was open for 4% -> 43% of each run, Pallas kernels for 0% -> 0%
where the time goes in v1:
time: 837 us; the launch traced here: 830 us
  waiting for transfers between devices  263 us (31%)
  matrix products  213 us (25%)
  local copies, waits for them, and re-layouts  164 us (20%)
  starting transfers between devices  122 us (15%)
  other arithmetic  52.4 us (6%)
  between operations  15.8 us (2%)
    ppermute x59, waiting for transfers between devices, shifted(): return lax.ppermute(x, axis, [(i, (i + k) % size) for i in range(size)])  263 us
    ppermute x59, starting transfers between devices, shifted(): return lax.ppermute(x, axis, [(i, (i + k) % size) for i in range(size)])  122 us
    dot_general x16, matrix products, body(): jnp.einsum('gpc,qgdc->pqd', pairs[l][:, b], weights[l], preferred_element...  84 us
    dynamic_slice x66, local copies, waits for them, and re-layouts, pick(): lax.dynamic_slice_in_dim(term, (s * heads + h) * width, width, axis=1)  64.7 us
    dot_general x4, matrix products, body(): jnp.einsum('bpqd,qgdc->gbpc', source, weights[l], preferred_element_type=...  55.9 us
    unnamed x216, local copies, waits for them, and re-layouts  27.2 us
    dynamic_update_slice x19, local copies, waits for them, and re-layouts, gathered(): lax.dynamic_update_index_in_dim(full, block, lax.rem(me - k + size, size)...  25.1 us
    dot_general x4, matrix products, body(): jnp.einsum('bgtd,gbpd->gbtp', grad_all[l], value, preferred_element_type=...  20.1 us
  transfers between devices with their start and end apart: 64, of which 22 were waited for; matrix products, arithmetic and copies ran while one was open for 43% of the time, Pallas kernels for 0%

profile of v1, /device:TPU:0, one launch (start us, length us, event | category | flops | bytes accessed | tf_op | source)
XLA Modules:
  0.0 830.2 jit_solution(18152015110908615828)
XLA Ops:
  21.5 18.9 %collective-permute-done.10 = bf16[2048,256]{0,1:T(8,128)(2,1)} collective-permute-done((bf16[2048,256]{0,1:T(8,128)(2,1)}, bf16[2048,256]{0,1:T(8,128)(2,1)}, u32[]{:S(2)}, u32[]{:S(2)}) %collective-permute-start.10) | collective-permute-done | bytes 1048608 | tf_op jit(solution)/shard_map/ppermute | solution.py:11
  42.7 19.3 %collective-permute-done.11 = bf16[2048,256]{0,1:T(8,128)(2,1)} collective-permute-done((bf16[2048,256]{0,1:T(8,128)(2,1)}, bf16[2048,256]{0,1:T(8,128)(2,1)}, u32[]{:S(2)}, u32[]{:S(2)}) %collective-permute-start.11) | collective-permute-done | bytes 1048608 | tf_op jit(solution)/shard_map/ppermute | solution.py:11
  78.7 18.2 %collective-permute-done = bf16[2,4,4,128,128]{4,3,1,2,0:T(8,128)(2,1)S(1)} collective-permute-done((bf16[2,4,4,128,128]{4,3,1,2,0:T(8,128)(2,1)S(1)}, bf16[2,4,4,128,128]{4,3,1,2,0:T(8,128)(2,1)S(1)}, u32[]{:S(2)}, u32[]{:S(2)}) %collective-permute-start) | collective-permute-done | bytes 1048608 | tf_op jit(solution)/shard_map/ppermute | solution.py:11
  97.9 19.6 %collective-permute-done.1 = bf16[2,4,4,128,128]{4,3,1,2,0:T(8,128)(2,1)S(1)} collective-permute-done((bf16[2,4,4,128,128]{4,3,1,2,0:T(8,128)(2,1)S(1)}, bf16[2,4,4,128,128]{4,3,1,2,0:T(8,128)(2,1)S(1)}, u32[]{:S(2)}, u32[]{:S(2)}) %collective-permute-start.1) | collective-permute-done | bytes 1048608 | tf_op jit(solution)/shard_map/ppermute | solution.py:11
  129.3 19.1 %collective-permute-done.17 = bf16[2048,256]{0,1:T(8,128)(2,1)S(1)} collective-permute-done((bf16[2048,256]{0,1:T(8,128)(2,1)}, bf16[2048,256]{0,1:T(8,128)(2,1)S(1)}, u32[]{:S(2)}, u32[]{:S(2)}) %collective-permute-start.17) | collective-permute-done | bytes 1048608 | tf_op jit(solution)/shard_map/ppermute | solution.py:11
  149.4 19.4 %collective-permute-done.18 = bf16[2048,256]{0,1:T(8,128)(2,1)S(1)} collective-permute-done((bf16[2048,256]{0,1:T(8,128)(2,1)}, bf16[2048,256]{0,1:T(8,128)(2,1)S(1)}, u32[]{:S(2)}, u32[]{:S(2)}) %collective-permute-start.18) | collective-permute-done | bytes 1048608 | tf_op jit(solution)/shard_map/ppermute | solution.py:11
  180.0 18.8 %collective-permute-done.3 = bf16[2048,256]{0,1:T(8,128)(2,1)S(1)} collective-permute-done((bf16[2048,256]{0,1:T(8,128)(2,1)S(1)}, bf16[2048,256]{0,1:T(8,128)(2,1)S(1)}, u32[]{:S(2)}, u32[]{:S(2)}) %collective-permute-start.3) | collective-permute-done | bytes 1048608 | tf_op jit(solution)/shard_map/ppermute | solution.py:11
  199.8 19.6 %collective-permute-done.4 = bf16[2048,256]{0,1:T(8,128)(2,1)S(1)} collective-permute-done((bf16[2048,256]{0,1:T(8,128)(2,1)S(1)}, bf16[2048,256]{0,1:T(8,128)(2,1)S(1)}, u32[]{:S(2)}, u32[]{:S(2)}) %collective-permute-start.4) | collective-permute-done | bytes 1048608 | tf_op jit(solution)/shard_map/ppermute | solution.py:11
  227.1 9.5 %constant_dynamic-slice_fusion.80 = bf16[4,256,4096]{2,1,0:T(8,128)(2,1)} fusion(bf16[4,1024,4096]{2,1,0:T(8,128)(2,1)} %param.6, s32[]{:T(128)S(6)} %select_n.214), kind=kLoop, calls=%fused_computation.346 | loop fusion | bytes 16777220 | tf_op jit(solution)/shard_map/dynamic_slice | solution.py:74
  240.4 12.0 %copy.457 = bf16[4,256,4096]{1,2,0:T(8,128)(2,1)} copy(bf16[4,256,4096]{2,1,0:T(8,128)(2,1)} %constant_dynamic-slice_fusion.80) | data formatting | bytes 16777216
  254.7 15.2 %collective-permute-done.25 = bf16[2048,256]{0,1:T(8,128)(2,1)S(1)} collective-permute-done((bf16[2048,256]{0,1:T(8,128)(2,1)S(1)}, bf16[2048,256]{0,1:T(8,128)(2,1)S(1)}, u32[]{:S(2)}, u32[]{:S(2)}) %collective-permute-start.25) | collective-permute-done | bytes 1048608 | tf_op jit(solution)/shard_map/ppermute | solution.py:11
  272.1 13.7 %fusion.30 = bf16[4,4,256,256]{2,3,1,0:T(8,128)(2,1)S(1)} fusion(bf16[4,256,2,2048,1]{1,3,2,0,4:T(8,128)(2,1)} %bitcast.1114, bf16[2,4,2048,256]{2,3,0,1:T(8,128)(2,1)} %all-gather.10.cloned.1.call-done), kind=kOutput, calls=%fused_computation.97 | convolution fusion | flops 8590983168 | bytes 18874368 | tf_op jit(solution)/shard_map/bpqd,qgdc->gbpc/dot_general | solution.py:81
  285.8 4.8 fusion.55
  290.6 13.7 %fusion.33 = bf16[4,4,256,256]{2,3,1,0:T(8,128)(2,1)S(1)} fusion(bf16[4,256,2,2048,1]{1,3,2,0,4:T(8,128)(2,1)} %bitcast.1115, bf16[2,4,2048,256]{2,3,0,1:T(8,128)(2,1)} %all-gather.12.cloned.1.call-done), kind=kOutput, calls=%fused_computation.98 | convolution fusion | flops 8590983168 | bytes 18874368 | tf_op jit(solution)/shard_map/bpqd,qgdc->gbpc/dot_general | solution.py:81
  309.6 14.2 %fusion.27 = bf16[4,4,256,256]{2,3,1,0:T(8,128)(2,1)S(1)} fusion(bf16[4,256,2,2048,1]{1,3,2,0,4:T(8,128)(2,1)} %bitcast.1116, bf16[2,4,2048,256]{2,3,0,1:T(8,128)(2,1)} %all-gather.8.cloned.1.call-done), kind=kOutput, calls=%fused_computation.96 | convolution fusion | flops 8590983168 | bytes 18874368 | tf_op jit(solution)/shard_map/bpqd,qgdc->gbpc/dot_general | solution.py:81
  323.8 14.4 %fusion.36 = bf16[4,4,256,256]{2,3,1,0:T(8,128)(2,1)S(1)} fusion(bf16[4,256,2,2048,1]{1,3,2,0,4:T(8,128)(2,1)} %bitcast.1117, bf16[2,4,2048,256]{2,3,0,1:T(8,128)(2,1)} %all-gather.14.cloned.1.call-done), kind=kOutput, calls=%fused_computation.99 | convolution fusion | flops 8590983168 | bytes 18874368 | tf_op jit(solution)/shard_map/bpqd,qgdc->gbpc/dot_general | solution.py:81
  343.6 8.3 %fusion.47 = (f32[4,4,256]{2,1,0:T(4,128)S(1)}, f32[4,4,256]{2,1,0:T(4,128)S(1)}, f32[4,4,256]{2,1,0:T(4,128)S(1)}, f32[4,4,256]{2,1,0:T(4,128)S(1)}, f32[4,4,256]{2,1,0:T(4,128)S(1)}, /*index=5*/f32[4,4,256,256]{2,3,1,0:T(8,128)}) fusion(f32[4,4,256]{2,1,0:T(4,128)S(1)} %get-tuple-element.131, f32[4,4,256,256]{2,3,1,0:T(8,128)S(1)} %get-tuple-element.132, ...), kind=kOutput, calls=%fused_computation.116 | convolution fusion | flops 284143616 | bytes 23168000 | tf_op jit(solution)/shard_map/bgtd,gbpd->gbtp/dot_general | solution.py:89
  356.4 7.5 fusion.48
  393.1 9.7 %multiply_convert_fusion.3 = (bf16[4,4,256,256]{2,3,1,0:T(8,128)(2,1)}, bf16[4,4,256,256]{2,3,1,0:T(8,128)(2,1)}, bf16[4,4,256,256]{2,3,1,0:T(8,128)(2,1)}) fusion(f32[4,4,256,256]{2,3,1,0:T(8,128)} %get-tuple-element.133, f32[4,4,256]{2,1,0:T(4,128)} %fusion.178, f32[4,4,256]{2,1,0:T(4,128)} %copy-done.90, f32[4,4,256]{2,1,0:T(4,128)} %copy-done.40, ...), kind=kLoop, calls=%fused_computation.42 | loop fusion | flops 22020096 | bytes 31605760 | tf_op jit(solution)/shard_map/convert_element_type | solution.py:103
  492.5 11.3 %fusion.8 = bf16[256,2,2048]{2,0,1:T(8,128)(2,1)} fusion(f32[256,2,2048,1]{2,0,1,3:T(8,128)} %fusion.126, f32[256,2,2048,1]{2,0,1,3:T(8,128)} %fusion.130, f32[256,2,2048,1]{2,0,1,3:T(8,128)} %fusion.134, bf16[2,4,2048,256]{2,3,0,1:T(8,128)(2,1)} %all-gather.14.cloned.1.call-done, bf16[4,4,256,128]{3,2,1,0:T(8,128)(2,1)S(1)} %copy-done.96, ...), kind=kOutput, calls=%fused_computation.11 | convolution fusion | flops 2152726528 | bytes 25165824 | tf_op jit(solution)/shard_map/gpc,qgdc->pqd/dot_general | solution.py:121
  503.8 8.6 %fusion.9 = bf16[256,2,2048]{2,0,1:T(8,128)(2,1)} fusion(f32[256,2,2048,1]{2,0,1,3:T(8,128)S(1)} %fusion.88, f32[256,2,2048,1]{2,0,1,3:T(8,128)S(1)} %copy-done.2, f32[256,2,2048,1]{2,0,1,3:T(8,128)} %fusion.112, bf16[2,4,2048,256]{2,3,0,1:T(8,128)(2,1)} %all-gather.14.cloned.1.call-done, bf16[4,4,256,128]{3,2,1,0:T(8,128)(2,1)S(1)} %copy-done.97, ...), kind=kOutput, calls=%fused_computation.15 | convolution fusion | flops 2152726528 | bytes 25165824 | tf_op jit(solution)/shard_map/gpc,qgdc->pqd/dot_general | solution.py:121
  512.3 10.2 %fusion.10 = bf16[256,2,2048]{2,0,1:T(8,128)(2,1)} fusion(f32[256,2,2048,1]{2,0,1,3:T(8,128)S(1)} %copy-done.3, f32[256,2,2048,1]{2,0,1,3:T(8,128)} %fusion.108, f32[256,2,2048,1]{2,0,1,3:T(8,128)} %fusion.120, bf16[2,4,2048,256]{2,3,0,1:T(8,128)(2,1)} %all-gather.14.cloned.1.call-done, bf16[4,4,256,128]{3,2,1,0:T(8,128)(2,1)S(1)} %copy-done.97, ...), kind=kOutput, calls=%fused_computation.19 | convolution fusion | flops 2152726528 | bytes 25165824 | tf_op jit(solution)/shard_map/gpc,qgdc->pqd/dot_general | solution.py:121
  522.6 7.2 fusion.11
  624.4 21.2 %collective-permute-done.36 = bf16[4,256,256]{2,1,0:T(8,128)(2,1)} collective-permute-done((bf16[4,256,256]{2,1,0:T(8,128)(2,1)}, bf16[4,256,256]{2,1,0:T(8,128)(2,1)}, u32[]{:S(2)}, u32[]{:S(2)}) %collective-permute-start.36) | collective-permute-done | bytes 524320 | tf_op jit(solution)/shard_map/ppermute | solution.py:11
  668.1 23.6 %collective-permute-start.47 = (bf16[4,256,256]{2,1,0:T(8,128)(2,1)S(1)}, bf16[4,256,256]{2,1,0:T(8,128)(2,1)S(1)}, u32[]{:S(2)}, u32[]{:S(2)}) collective-permute-start(bf16[4,256,256]{2,1,0:T(8,128)(2,1)S(1)} %pad_maximum_fusion.11), channel_id=1, source_target_pairs={{0,1},{1,2},{2,3},{3,0},{4,5},{5,6},{6,7},{7,4},{8,9},{9,10},{10,1... | collective-permute-start | bytes 1572872 | tf_op jit(solution)/shard_map/ppermute | solution.py:11
  707.0 6.0 collective-permute-done.48
  721.3 20.6 %collective-permute-start.53 = (bf16[4,256,256]{2,1,0:T(8,128)(2,1)S(1)}, bf16[4,256,256]{2,1,0:T(8,128)(2,1)S(1)}, u32[]{:S(2)}, u32[]{:S(2)}) collective-permute-start(bf16[4,256,256]{2,1,0:T(8,128)(2,1)S(1)} %copy-done.69), channel_id=1, source_target_pairs={{0,1},{1,2},{2,3},{3,0},{4,5},{5,6},{6,7},{7,4},{8,9},{9,10},{10,1... | collective-permute-start | bytes 1572872 | tf_op jit(solution)/shard_map/ppermute | solution.py:11
  742.1 4.8 collective-permute-start.50
  748.4 5.3 add_convert_fusion
  761.3 42.8 %collective-permute-done.52 = bf16[1,256,256]{2,1,0:T(8,128)(2,1)S(1)} collective-permute-done((bf16[1,256,256]{2,1,0:T(8,128)(2,1)S(1)}, bf16[1,256,256]{2,1,0:T(8,128)(2,1)S(1)}, u32[]{:S(2)}, u32[]{:S(2)}) %collective-permute-start.52) | collective-permute-done | bytes 131104 | tf_op jit(solution)/shard_map/ppermute | solution.py:11
  806.6 5.7 collective-permute-done.56
  812.6 4.8 collective-permute-done.58
  (529 shorter events, 366.6 us)
Async XLA Ops:
  7.2 264.9 %all-gather.10.cloned.1.call-start = ((), (), s32[]{:S(2)}) async-start(), calls=%async_computation.2 | async-start | bytes 12582912 | tf_op jit(solution)/shard_map/all_gather | solution.py:72
  15.0 47.0 %collective-permute-start.11 = (bf16[2048,256]{0,1:T(8,128)(2,1)}, bf16[2048,256]{0,1:T(8,128)(2,1)}, u32[]{:S(2)}, u32[]{:S(2)}) collective-permute-start(bf16[2048,256]{0,1:T(8,128)(2,1)} %bitcast.1122), channel_id=1, source_target_pairs={{0,16},{8,24},{16,0},{24,8},{1,17},{9,25},{17,1},{25,9},{2,18},{10... | collective-permute-start | bytes 3145736 | tf_op jit(solution)/shard_map/ppermute | solution.py:11
  16.5 47.8 %collective-permute-start.12 = (bf16[2048,256]{0,1:T(8,128)(2,1)}, bf16[2048,256]{0,1:T(8,128)(2,1)}, u32[]{:S(2)}, u32[]{:S(2)}) collective-permute-start(bf16[2048,256]{0,1:T(8,128)(2,1)} %bitcast.1123), channel_id=1, source_target_pairs={{0,24},{8,0},{16,8},{24,16},{1,25},{9,1},{17,9},{25,17},{2,26},{10... | collective-permute-start | bytes 3145736 | tf_op jit(solution)/shard_map/ppermute | solution.py:11
  66.7 219.1 %all-gather.6.cloned.1.call-start = ((), (), s32[]{:S(2)}) async-start(), calls=%async_computation | async-start | bytes 12582912 | tf_op jit(solution)/shard_map/all_gather | solution.py:64
  71.7 45.7 %collective-permute-start.1 = (bf16[2,4,4,128,128]{4,3,1,2,0:T(8,128)(2,1)S(1)}, bf16[2,4,4,128,128]{4,3,1,2,0:T(8,128)(2,1)S(1)}, u32[]{:S(2)}, u32[]{:S(2)}) collective-permute-start(bf16[2,4,4,128,128]{4,3,1,2,0:T(8,128)(2,1)S(1)} %fusion.225), channel_id=1, source_target_pairs={{0,16},{8,24},{16,0},{24,8},{1,17},{9,25},{17,1},{25,9},{2,18},{10... | collective-permute-start | bytes 3145736 | tf_op jit(solution)/shard_map/ppermute | solution.py:11
  71.7 46.8 %collective-permute-start.2 = (bf16[2,4,4,128,128]{4,3,1,2,0:T(8,128)(2,1)S(1)}, bf16[2,4,4,128,128]{4,3,1,2,0:T(8,128)(2,1)S(1)}, u32[]{:S(2)}, u32[]{:S(2)}) collective-permute-start(bf16[2,4,4,128,128]{4,3,1,2,0:T(8,128)(2,1)S(1)} %fusion.225), channel_id=1, source_target_pairs={{0,24},{8,0},{16,8},{24,16},{1,25},{9,1},{17,9},{25,17},{2,26},{10... | collective-permute-start | bytes 3145736 | tf_op jit(solution)/shard_map/ppermute | solution.py:11
  119.6 170.9 %all-gather.12.cloned.1.call-start = ((), (), s32[]{:S(2)}) async-start(), calls=%async_computation.3 | async-start | bytes 12582912 | tf_op jit(solution)/shard_map/all_gather | solution.py:72
  123.8 45.1 %collective-permute-start.18 = (bf16[2048,256]{0,1:T(8,128)(2,1)}, bf16[2048,256]{0,1:T(8,128)(2,1)S(1)}, u32[]{:S(2)}, u32[]{:S(2)}) collective-permute-start(bf16[2048,256]{0,1:T(8,128)(2,1)} %bitcast.1125), channel_id=1, source_target_pairs={{0,16},{8,24},{16,0},{24,8},{1,17},{9,25},{17,1},{25,9},{2,18},{10... | collective-permute-start | bytes 3145736 | tf_op jit(solution)/shard_map/ppermute | solution.py:11
  124.2 45.8 %collective-permute-start.19 = (bf16[2048,256]{0,1:T(8,128)(2,1)}, bf16[2048,256]{0,1:T(8,128)(2,1)S(1)}, u32[]{:S(2)}, u32[]{:S(2)}) collective-permute-start(bf16[2048,256]{0,1:T(8,128)(2,1)} %bitcast.1126), channel_id=1, source_target_pairs={{0,24},{8,0},{16,8},{24,16},{1,25},{9,1},{17,9},{25,17},{2,26},{10... | collective-permute-start | bytes 3145736 | tf_op jit(solution)/shard_map/ppermute | solution.py:11
  171.0 138.6 %all-gather.8.cloned.1.call-start = ((), (), s32[]{:S(2)}) async-start(), calls=%async_computation.1 | async-start | bytes 12582912 | tf_op jit(solution)/shard_map/all_gather | solution.py:72
  173.7 45.7 %collective-permute-start.4 = (bf16[2048,256]{0,1:T(8,128)(2,1)S(1)}, bf16[2048,256]{0,1:T(8,128)(2,1)S(1)}, u32[]{:S(2)}, u32[]{:S(2)}) collective-permute-start(bf16[2048,256]{0,1:T(8,128)(2,1)S(1)} %bitcast.1128), channel_id=1, source_target_pairs={{0,16},{8,24},{16,0},{24,8},{1,17},{9,25},{17,1},{25,9},{2,18},{10... | collective-permute-start | bytes 3145736 | tf_op jit(solution)/shard_map/ppermute | solution.py:11
  173.7 46.8 %collective-permute-start.5 = (bf16[2048,256]{0,1:T(8,128)(2,1)S(1)}, bf16[2048,256]{0,1:T(8,128)(2,1)S(1)}, u32[]{:S(2)}, u32[]{:S(2)}) collective-permute-start(bf16[2048,256]{0,1:T(8,128)(2,1)S(1)} %bitcast.1129), channel_id=1, source_target_pairs={{0,24},{8,0},{16,8},{24,16},{1,25},{9,1},{17,9},{25,17},{2,26},{10... | collective-permute-start | bytes 3145736 | tf_op jit(solution)/shard_map/ppermute | solution.py:11
  221.6 102.2 %all-gather.14.cloned.1.call-start = ((), (), s32[]{:S(2)}) async-start(), calls=%async_computation.4 | async-start | bytes 12582912 | tf_op jit(solution)/shard_map/all_gather | solution.py:72
  225.0 44.9 %collective-permute-start.25 = (bf16[2048,256]{0,1:T(8,128)(2,1)S(1)}, bf16[2048,256]{0,1:T(8,128)(2,1)S(1)}, u32[]{:S(2)}, u32[]{:S(2)}) collective-permute-start(bf16[2048,256]{0,1:T(8,128)(2,1)S(1)} %bitcast.1119), channel_id=1, source_target_pairs={{0,16},{8,24},{16,0},{24,8},{1,17},{9,25},{17,1},{25,9},{2,18},{10... | collective-permute-start | bytes 3145736 | tf_op jit(solution)/shard_map/ppermute | solution.py:11
  225.4 45.6 %collective-permute-start.26 = (bf16[2048,256]{0,1:T(8,128)(2,1)S(1)}, bf16[2048,256]{0,1:T(8,128)(2,1)S(1)}, u32[]{:S(2)}, u32[]{:S(2)}) collective-permute-start(bf16[2048,256]{0,1:T(8,128)(2,1)S(1)} %bitcast.1120), channel_id=1, source_target_pairs={{0,24},{8,0},{16,8},{24,16},{1,25},{9,1},{17,9},{25,17},{2,26},{10... | collective-permute-start | bytes 3145736 | tf_op jit(solution)/shard_map/ppermute | solution.py:11
  423.3 323.6 %collective-permute-start.31 = (bf16[4,2,4,4,128,128]{5,4,3,2,1,0:T(8,128)(2,1)}, bf16[4,2,4,4,128,128]{5,4,3,2,1,0:T(8,128)(2,1)}, u32[]{:S(2)}, u32[]{:S(2)}) collective-permute-start(bf16[4,2,4,4,128,128]{5,4,3,2,1,0:T(8,128)(2,1)} %constant_dynamic-slice_fusion.79), channel_id=1, source_target_pairs={{0,4},{4,0},{1,5},{5,1},{2,6},{6,2},{3,7},{7,3},{8,12},{12,8},{9,1... | collective-permute-start | bytes 12582920 | tf_op jit(solution)/shard_map/ppermute | solution.py:11
  573.4 88.3 %collective-permute-start.43 = (bf16[4,256,256]{2,1,0:T(8,128)(2,1)}, bf16[4,256,256]{2,1,0:T(8,128)(2,1)}, u32[]{:S(2)}, u32[]{:S(2)}) collective-permute-start(bf16[4,256,256]{2,1,0:T(8,128)(2,1)} %pad_maximum_fusion.10), channel_id=1, source_target_pairs={{0,3},{1,0},{2,1},{3,2},{4,7},{5,4},{6,5},{7,6},{8,11},{9,8},{10,9... | collective-permute-start | bytes 1572872 | tf_op jit(solution)/shard_map/ppermute | solution.py:11
  583.7 37.8 %collective-permute-start.37 = (bf16[4,256,256]{2,1,0:T(8,128)(2,1)}, bf16[4,256,256]{2,1,0:T(8,128)(2,1)}, u32[]{:S(2)}, u32[]{:S(2)}) collective-permute-start(bf16[4,256,256]{2,1,0:T(8,128)(2,1)} %pad_maximum_fusion.7), channel_id=1, source_target_pairs={{0,3},{1,0},{2,1},{3,2},{4,7},{5,4},{6,5},{7,6},{8,11},{9,8},{10,9... | collective-permute-start | bytes 1572872 | tf_op jit(solution)/shard_map/ppermute | solution.py:11
  588.6 56.9 %collective-permute-start.36 = (bf16[4,256,256]{2,1,0:T(8,128)(2,1)}, bf16[4,256,256]{2,1,0:T(8,128)(2,1)}, u32[]{:S(2)}, u32[]{:S(2)}) collective-permute-start(bf16[4,256,256]{2,1,0:T(8,128)(2,1)} %pad_maximum_fusion.6), channel_id=1, source_target_pairs={{0,2},{1,3},{2,0},{3,1},{4,6},{5,7},{6,4},{7,5},{8,10},{9,11},{10,... | collective-permute-start | bytes 1572872 | tf_op jit(solution)/shard_map/ppermute | solution.py:11
  593.7 51.9 %collective-permute-start.35 = (bf16[4,256,256]{2,1,0:T(8,128)(2,1)}, bf16[4,256,256]{2,1,0:T(8,128)(2,1)}, u32[]{:S(2)}, u32[]{:S(2)}) collective-permute-start(bf16[4,256,256]{2,1,0:T(8,128)(2,1)} %pad_maximum_fusion.5), channel_id=1, source_target_pairs={{0,1},{1,2},{2,3},{3,0},{4,5},{5,6},{6,7},{7,4},{8,9},{9,10},{10,1... | collective-permute-start | bytes 1572872 | tf_op jit(solution)/shard_map/ppermute | solution.py:11
  621.5 46.6 %collective-permute-start.42 = (bf16[4,256,256]{2,1,0:T(8,128)(2,1)}, bf16[4,256,256]{2,1,0:T(8,128)(2,1)}, u32[]{:S(2)}, u32[]{:S(2)}) collective-permute-start(bf16[4,256,256]{2,1,0:T(8,128)(2,1)} %pad_maximum_fusion.9), channel_id=1, source_target_pairs={{0,2},{1,3},{2,0},{3,1},{4,6},{5,7},{6,4},{7,5},{8,10},{9,11},{10,... | collective-permute-start | bytes 1572872 | tf_op jit(solution)/shard_map/ppermute | solution.py:11
  648.2 43.5 %collective-permute-start.38 = (bf16[1,256,256]{2,1,0:T(8,128)(2,1)}, bf16[1,256,256]{2,1,0:T(8,128)(2,1)}, u32[]{:S(2)}, u32[]{:S(2)}) collective-permute-start(bf16[1,256,256]{2,1,0:T(8,128)(2,1)} %get-tuple-element.114), channel_id=1, source_target_pairs={{0,8},{8,16},{16,24},{24,0},{1,9},{9,17},{17,25},{25,1},{2,10},{10... | collective-permute-start | bytes 393224 | tf_op jit(solution)/shard_map/ppermute | solution.py:11
  661.7 41.3 %collective-permute-start.49 = (bf16[4,256,256]{2,1,0:T(8,128)(2,1)}, bf16[4,256,256]{2,1,0:T(8,128)(2,1)S(1)}, u32[]{:S(2)}, u32[]{:S(2)}) collective-permute-start(bf16[4,256,256]{2,1,0:T(8,128)(2,1)} %pad_maximum_fusion.13), channel_id=1, source_target_pairs={{0,3},{1,0},{2,1},{3,2},{4,7},{5,4},{6,5},{7,6},{8,11},{9,8},{10,9... | collective-permute-start | bytes 1572872 | tf_op jit(solution)/shard_map/ppermute | solution.py:11
  668.1 44.9 %collective-permute-start.48 = (bf16[4,256,256]{2,1,0:T(8,128)(2,1)}, bf16[4,256,256]{2,1,0:T(8,128)(2,1)S(1)}, u32[]{:S(2)}, u32[]{:S(2)}) collective-permute-start(bf16[4,256,256]{2,1,0:T(8,128)(2,1)} %pad_maximum_fusion.12), channel_id=1, source_target_pairs={{0,2},{1,3},{2,0},{3,1},{4,6},{5,7},{6,4},{7,5},{8,10},{9,11},{10,... | collective-permute-start | bytes 1572872 | tf_op jit(solution)/shard_map/ppermute | solution.py:11
  668.1 46.8 %collective-permute-start.47 = (bf16[4,256,256]{2,1,0:T(8,128)(2,1)S(1)}, bf16[4,256,256]{2,1,0:T(8,128)(2,1)S(1)}, u32[]{:S(2)}, u32[]{:S(2)}) collective-permute-start(bf16[4,256,256]{2,1,0:T(8,128)(2,1)S(1)} %pad_maximum_fusion.11), channel_id=1, source_target_pairs={{0,1},{1,2},{2,3},{3,0},{4,5},{5,6},{6,7},{7,4},{8,9},{9,10},{10,1... | collective-permute-start | bytes 1572872 | tf_op jit(solution)/shard_map/ppermute | solution.py:11
  702.7 52.6 %collective-permute-start.55 = (bf16[4,256,256]{2,1,0:T(8,128)(2,1)S(1)}, bf16[4,256,256]{2,1,0:T(8,128)(2,1)S(1)}, u32[]{:S(2)}, u32[]{:S(2)}) collective-permute-start(bf16[4,256,256]{2,1,0:T(8,128)(2,1)S(1)} %copy-done.68), channel_id=1, source_target_pairs={{0,3},{1,0},{2,1},{3,2},{4,7},{5,4},{6,5},{7,6},{8,11},{9,8},{10,9... | collective-permute-start | bytes 1572872 | tf_op jit(solution)/shard_map/ppermute | solution.py:11
  703.0 54.4 %collective-permute-start.54 = (bf16[4,256,256]{2,1,0:T(8,128)(2,1)S(1)}, bf16[4,256,256]{2,1,0:T(8,128)(2,1)S(1)}, u32[]{:S(2)}, u32[]{:S(2)}) collective-permute-start(bf16[4,256,256]{2,1,0:T(8,128)(2,1)S(1)} %copy-done.67), channel_id=1, source_target_pairs={{0,2},{1,3},{2,0},{3,1},{4,6},{5,7},{6,4},{7,5},{8,10},{9,11},{10,... | collective-permute-start | bytes 1572872 | tf_op jit(solution)/shard_map/ppermute | solution.py:11
  721.3 36.6 %collective-permute-start.53 = (bf16[4,256,256]{2,1,0:T(8,128)(2,1)S(1)}, bf16[4,256,256]{2,1,0:T(8,128)(2,1)S(1)}, u32[]{:S(2)}, u32[]{:S(2)}) collective-permute-start(bf16[4,256,256]{2,1,0:T(8,128)(2,1)S(1)} %copy-done.69), channel_id=1, source_target_pairs={{0,1},{1,2},{2,3},{3,0},{4,5},{5,6},{6,7},{7,4},{8,9},{9,10},{10,1... | collective-permute-start | bytes 1572872 | tf_op jit(solution)/shard_map/ppermute | solution.py:11
  755.3 62.1 %collective-permute-start.34 = (bf16[2,4,4,128,128]{4,3,2,1,0:T(8,128)(2,1)}, bf16[2,4,4,128,128]{4,3,2,1,0:T(8,128)(2,1)}, u32[]{:S(2)}, u32[]{:S(2)}) collective-permute-start(bf16[2,4,4,128,128]{4,3,2,1,0:T(8,128)(2,1)} %get-tuple-element.32), channel_id=1, source_target_pairs={{0,24},{8,0},{16,8},{24,16},{1,25},{9,1},{17,9},{25,17},{2,26},{10... | collective-permute-start | bytes 3145736 | tf_op jit(solution)/shard_map/ppermute | solution.py:11
  757.4 60.0 %collective-permute-start.33 = (bf16[2,4,4,128,128]{4,3,2,1,0:T(8,128)(2,1)}, bf16[2,4,4,128,128]{4,3,2,1,0:T(8,128)(2,1)}, u32[]{:S(2)}, u32[]{:S(2)}) collective-permute-start(bf16[2,4,4,128,128]{4,3,2,1,0:T(8,128)(2,1)} %get-tuple-element.33), channel_id=1, source_target_pairs={{0,16},{8,24},{16,0},{24,8},{1,17},{9,25},{17,1},{25,9},{2,18},{10... | collective-permute-start | bytes 3145736 | tf_op jit(solution)/shard_map/ppermute | solution.py:11
  758.0 59.4 %collective-permute-start.32 = (bf16[2,4,4,128,128]{4,3,2,1,0:T(8,128)(2,1)S(1)}, bf16[2,4,4,128,128]{4,3,2,1,0:T(8,128)(2,1)}, u32[]{:S(2)}, u32[]{:S(2)}) collective-permute-start(bf16[2,4,4,128,128]{4,3,2,1,0:T(8,128)(2,1)S(1)} %get-tuple-element.31), channel_id=1, source_target_pairs={{0,8},{8,16},{16,24},{24,0},{1,9},{9,17},{17,25},{25,1},{2,10},{10... | collective-permute-start | bytes 3145736 | tf_op jit(solution)/shard_map/ppermute | solution.py:11
  761.1 43.0 %collective-permute-start.52 = (bf16[1,256,256]{2,1,0:T(8,128)(2,1)S(1)}, bf16[1,256,256]{2,1,0:T(8,128)(2,1)S(1)}, u32[]{:S(2)}, u32[]{:S(2)}) collective-permute-start(bf16[1,256,256]{2,1,0:T(8,128)(2,1)S(1)} %get-tuple-element.104), channel_id=1, source_target_pairs={{0,24},{8,0},{16,8},{24,16},{1,25},{9,1},{17,9},{25,17},{2,26},{10... | collective-permute-start | bytes 393224 | tf_op jit(solution)/shard_map/ppermute | solution.py:11
  (136 other events, 1855.2 us)
Sparse Core Ops, SparseCore 0:
  66.8 20.5 all-gather.9
  119.7 21.3 all-gather.5
  171.2 20.5 all-gather.11
  221.7 21.2 all-gather.7
  272.2 20.4 all-gather.13
